TPU v7x, 512 devices: a whole 4x4x16 slice. The times are simulated.
512 devices in a mesh: aux: 16 (over x, y), orb: 32 (over z, core).
Axes of the slice: x: 4, y: 4, z: 16, core: 2. Of those that a mesh axis runs over, the one named last changes fastest.
Arguments:
- tensor: bfloat16 [96, 64, 64, 2048], P('orb', None, None, 'aux'), may hold values from -6 to 6
- nu_index: int32 [32, 3], P('orb'), may hold values from 0 to 31, as said below
- density: bfloat16 [2048, 256], P(('aux', 'orb')), may hold values from -0.4375 to 0.4375
- density_pattern: int32 [32, 4], replicated, may hold values 0 or 1
- blockmap: int32 [32], replicated, may hold values from 0 to 31, each once
- virtual: bfloat16 [2048, 512], P(('aux', 'orb')), may hold values from -0.125 to 0.125
Outputs:
- three_index: bfloat16 [512, 256, 2048], P(None, 'orb', 'aux')
Inputs may be any that keep to these rules, and one draw needn't show every extreme that they name: `nu_index`: row r holds 3 different nu blocks, one of them r itself. `blockmap`: each mu block is held by exactly one index of orb.
All inputs are finite; a program needn't handle non-finite values.
Results may differ from a plain program's by a relative error of at most 0.0049.
Values may be sent and summed in bfloat16 or wider, within the bound.
A program may use at most 64 MiB of HBM per device.

v0:
```python
import jax
import jax.numpy as jnp
from jax import lax
from jax.sharding import PartitionSpec as P


def on_device(tensor, nu_index, density, density_pattern, blockmap, virtual):
    slot_count = tensor.shape[0]
    block_width = tensor.shape[1]
    p_local = tensor.shape[3]
    orb_count = lax.axis_size("orb")
    dens_full = lax.all_gather(density, ("aux", "orb"), axis=0, tiled=True)
    virt_full = lax.all_gather(virtual, ("aux", "orb"), axis=0, tiled=True)
    lam_total = dens_full.shape[1]
    kept_mask = (
        jnp.repeat(jnp.repeat(density_pattern, block_width, axis=0), block_width, axis=1) > 0
    )
    masked = jnp.where(kept_mask, dens_full, jnp.zeros_like(dens_full))
    row_blocks = [
        lax.dynamic_slice_in_dim(masked, nu_index[0, slot_index] * block_width, block_width, 0)
        for slot_index in range(slot_count)
    ]
    chosen = jnp.concatenate(row_blocks, 0)
    flattened = tensor.reshape(slot_count * block_width, block_width * p_local)
    half_done = lax.dot_general(
        chosen, flattened, (((0,), (0,)), ((), ())), preferred_element_type=jnp.float32
    )
    half_done = half_done.astype(jnp.bfloat16).reshape(lam_total, block_width, p_local)
    block_ids = jnp.arange(orb_count, dtype=jnp.int32)
    matches = blockmap[:, None] == block_ids[None, :]
    inverse = jnp.sum(jnp.where(matches, block_ids[:, None], 0), axis=0)
    remapped = lax.all_to_all(half_done, "orb", split_axis=0, concat_axis=1, tiled=True)
    lam_local = remapped.shape[0]
    p_items = remapped.shape[2]
    ordered = remapped.reshape(lam_local, orb_count, block_width, p_items)[:, inverse]
    ordered = ordered.reshape(lam_local, orb_count * block_width, p_items)
    accumulated = jnp.einsum("ms,lmp->slp", virt_full, ordered, preferred_element_type=jnp.float32)
    return accumulated.astype(jnp.bfloat16)


def solution(mesh):
    in_specs = (
        P("orb", None, None, "aux"),
        P("orb", None),
        P(("aux", "orb"), None),
        P(),
        P(),
        P(("aux", "orb"), None),
    )
    out_specs = P(None, "orb", "aux")
    return jax.shard_map(
        on_device, mesh=mesh, in_specs=in_specs, out_specs=out_specs, check_vma=False
    )
```

profile of v0, /device:TPU:1, one launch (start us, length us, event | category | flops | bytes accessed | tf_op | source)
XLA Modules:
  0.0 472.7 jit_solution(10852038430951148554)
XLA Ops:
  6.5 0.0 all-gather.5.cloned.1.call-start
  6.5 0.7 all-gather.5.cloned.1.call-update
  7.3 1.4 fusion.13
  10.5 0.7 broadcast_compare_fusion
  11.2 0.1 broadcast_in_dim.25
  11.3 0.1 gt.16
  11.4 173.9 %all-gather.5.cloned.1.call-done = bf16[512,4,256]{2,1,0:T(4,128)(2,1)} async-done(((bf16[1,4,256]{2,1,0:T(4,128)(2,1)}), bf16[512,4,256]{2,1,0:T(4,128)(2,1)}) %all-gather.5.cloned.1.call-update) | async-done | bytes 1048592 | tf_op jit(solution)/shard_map/all_gather | solution.py:12
  185.4 1.3 reshape.49
  186.7 0.6 copy.23
  187.4 0.1 bitcast_select_fusion
  187.5 0.1 constant_dynamic-slice_fusion.2
  187.6 4.4 fusion.2
  192.1 3.2 copy.30
  195.2 0.0 copy-start
  195.2 7.1 %all-to-all-start = ((bf16[256,64,128]{2,1,0:T(8,128)(2,1)}), bf16[256,64,128]{2,1,0:T(8,128)(2,1)}, u32[]{:S(2)}, u32[]{:S(2)}) async-start(bf16[256,64,128]{2,1,0:T(8,128)(2,1)} %bitcast.33), calls=%async_computation | async-start | bytes 8388608 | tf_op jit(solution)/shard_map/all_to_all | solution.py:32
  202.4 0.0 all-gather.7.cloned.1.call-start
  202.4 0.7 all-gather.7.cloned.1.call-update
  203.1 0.0 copy-done
  203.1 0.1 select_reduce_fusion
  203.2 242.3 %all-gather.7.cloned.1.call-done = bf16[512,4,512]{2,1,0:T(4,128)(2,1)} async-done(((bf16[1,4,512]{2,1,0:T(4,128)(2,1)}), bf16[512,4,512]{2,1,0:T(4,128)(2,1)}) %all-gather.7.cloned.1.call-update) | async-done | bytes 2097168 | tf_op jit(solution)/shard_map/all_gather | solution.py:13
  445.6 2.5 reshape.52
  448.1 0.0 all-to-all-done
  448.1 5.5 %copy.38 = bf16[32,8,64,128]{3,2,0,1:T(8,128)(2,1)} copy(bf16[32,8,64,128]{3,2,1,0:T(8,128)(2,1)} %bitcast.5) | data formatting | bytes 8388608 | tf_op jit(solution)/shard_map/all_to_all | solution.py:32
  453.6 5.2 %gather_fusion = bf16[32,8,64,128]{3,2,1,0:T(8,128)(2,1)} fusion(bf16[8,32,64,128]{3,2,1,0:T(8,128)(2,1)} %bitcast.34, s32[1024]{0:T(1024)S(1)} %pad_clamp_fusion), kind=kCustom, calls=%fused_computation | custom fusion | bytes 8388736 | tf_op jit(solution)/shard_map/gather | solution.py:35
  458.8 3.1 copy.25
  462.0 2.4 fusion.5
  464.4 1.5 copy.27
  (2 shorter events, 0.0 us)
Async XLA Ops:
  6.5 178.8 %all-gather.5.cloned.1.call-start = ((), (), s32[]{:S(2)}) async-start(), calls=%async_computation.1 | async-start | bytes 1050624 | tf_op jit(solution)/shard_map/all_gather | solution.py:12
  195.2 7.9 %copy-start = (s32[32]{0:T(128)S(1)}, s32[32]{0:T(128)}, u32[]{:S(2)}) copy-start(s32[32]{0:T(128)} %param.10) | copy-start | bytes 388
  195.2 252.9 %all-to-all-start = ((bf16[256,64,128]{2,1,0:T(8,128)(2,1)}), bf16[256,64,128]{2,1,0:T(8,128)(2,1)}, u32[]{:S(2)}, u32[]{:S(2)}) async-start(bf16[256,64,128]{2,1,0:T(8,128)(2,1)} %bitcast.33), calls=%async_computation | async-start | bytes 8388608 | tf_op jit(solution)/shard_map/all_to_all | solution.py:32
  202.4 243.2 %all-gather.7.cloned.1.call-start = ((), (), s32[]{:S(2)}) async-start(), calls=%async_computation.2 | async-start | bytes 2101248 | tf_op jit(solution)/shard_map/all_gather | solution.py:13
Sparse Core Ops, SparseCore 0:
  11.9 173.3 all-gather.4
  207.8 237.6 all-gather.6
where the time goes:
time: 473 us
  waiting for transfers between devices  418 us (88%)
  local copies, waits for them, and re-layouts  24.7 us (5%)
  between operations  15.4 us (3%)
  starting transfers between devices  7.16 us (2%)
  matrix products  6.79 us (1%)
    all_gather x1, waiting for transfers between devices, on_device(): virt_full = lax.all_gather(virtual, ('aux', 'orb'), axis=0, tiled=True)  242 us
    all_gather x1, waiting for transfers between devices, on_device(): dens_full = lax.all_gather(density, ('aux', 'orb'), axis=0, tiled=True)  174 us
  transfers between devices with their start and end apart: 3, of which 2 were waited for; matrix products, arithmetic and copies ran while one was open for 1% of the time, Pallas kernels for 0%

commit v1 on v0

v1 whole, which is shorter than its diff:
```python
import functools

import jax
import jax.numpy as jnp
from jax import lax
from jax.experimental import pallas as pl
from jax.experimental.pallas import tpu as pltpu
from jax.sharding import PartitionSpec as P

MESH = pl.DeviceIdType.MESH
BF16 = jnp.bfloat16
F32 = jnp.float32
BLK = 64
LANES = 128
REACH = 4
CHUNKS = 4
PAIR = 2


def kernel(
    aux_n, chips, nu_ref, pat_ref, bm_ref, dens_ref, virt_ref, t_hbm, out_ref,
    tbuf, big, tt, piece, d_in, d_all, v_all, d_sc, v_sc, d_nat, d_t, v_own, v_far,
    half, far, sib, part, hop,
    t_sem, a_snd, a_rcv, b_snd, b_rcv, c_snd, c_rcv, n_snd, n_rcv, f_snd, f_rcv, p_snd, p_rcv,
):
    aux = lax.axis_index("aux")
    orb = lax.axis_index("orb")
    chip = lax.div(orb, 2)
    core = lax.rem(orb, 2)
    other = 1 - core
    mate = (aux, 2 * chip + other)

    def ring(shift):
        return lax.rem(chip + shift + 2 * chips, chips)

    def remote(src, dst, snd, rcv, to):
        return pltpu.make_async_remote_copy(
            src_ref=src, dst_ref=dst, send_sem=snd, recv_sem=rcv, device_id=to, device_id_type=MESH
        )

    load_t = pltpu.make_async_copy(t_hbm, tbuf, t_sem)
    load_t.start()

    barrier = pltpu.get_barrier_semaphore()

    def greet(to):
        pl.semaphore_signal(barrier, inc=1, device_id=to, device_id_type=MESH)

    @pl.loop(1, chips)
    def _(i):
        greet((aux, 2 * ring(i) + core))

    @pl.loop(1, aux_n)
    def _(i):
        greet((lax.rem(aux + i, aux_n), orb))

    for j in range(1, REACH + 1):
        greet((aux, 2 * ring(j) + other))
        greet((aux, 2 * ring(-j) + other))
    greet(mate)

    dens = dens_ref[...].astype(F32)
    for b in range(2):
        d_in[chip, pl.ds(b, 4, stride=2), :] = dens[:, b * LANES : (b + 1) * LANES]
    virt = virt_ref[...].astype(F32)
    for b in range(4):
        piece[pl.ds(b, 4, stride=4), :] = virt[:, b * LANES : (b + 1) * LANES]
    span = chips // 2
    v_all[core, 2 * aux + lax.div(chip, span), lax.rem(chip, span)] = piece[...].astype(BF16)

    pl.semaphore_wait(barrier, (chips - 1) + (aux_n - 1) + 2 * REACH + 1)

    def d_along(i):
        return remote(d_in.at[chip], d_in.at[chip], a_snd.at[0, i], a_rcv.at[0, i], (aux, 2 * ring(i) + core))

    def v_along(i):
        mine = v_all.at[core, 2 * aux + lax.div(chip, span), lax.rem(chip, span)]
        return remote(mine, mine, a_snd.at[1, i], a_rcv.at[1, i], (aux, 2 * ring(i) + core))

    @pl.loop(1, chips)
    def _(i):
        d_along(i).start()

    @pl.loop(1, chips)
    def _(i):
        v_along(i).start()

    load_t.wait()

    @pl.loop(0, 3 * BLK // 8)
    def _(i):
        rows = tbuf[lax.div(i, 8), pl.ds(lax.rem(i, 8) * 8, 8)]
        big[pl.ds(pl.multiple_of(i * 512, 512), 512), :] = rows.astype(F32).reshape(512, LANES)

    @pl.loop(0, BLK)
    def _(m):
        tt[m] = big[pl.ds(m, 3 * BLK, stride=BLK), :].astype(BF16)

    @pl.loop(1, chips)
    def _(i):
        d_along(i).wait_recv()

    d_all[core, pl.ds(2 * aux, 2)] = d_in[...].reshape(2, BLK, LANES).astype(BF16)

    def d_plane(i):
        mine = d_all.at[core, pl.ds(2 * aux, 2)]
        return remote(mine, mine, b_snd.at[0, i], b_rcv.at[0, i], (lax.rem(aux + i, aux_n), orb))

    def v_plane(i):
        mine = v_all.at[core, pl.ds(2 * aux, 2)]
        return remote(mine, mine, b_snd.at[1, i], b_rcv.at[1, i], (lax.rem(aux + i, aux_n), orb))

    @pl.loop(1, aux_n)
    def _(i):
        d_plane(i).start()

    @pl.loop(1, chips)
    def _(i):
        v_along(i).wait_recv()

    @pl.loop(1, aux_n)
    def _(i):
        d_plane(i).wait_recv()

    d_mate = remote(d_all.at[core], d_all.at[core], c_snd.at[0], c_rcv.at[0], mate)
    v_mate = remote(v_all.at[core], v_all.at[core], c_snd.at[1], c_rcv.at[1], mate)
    d_mate.start()

    @pl.loop(1, aux_n)
    def _(i):
        v_plane(i).start()

    d_mate.wait_recv()

    lane = lax.broadcasted_iota(jnp.int32, (BLK, LANES), 1)
    d_nat[3 * BLK :, :] = jnp.zeros((BLK, 2 * LANES), F32)
    for s in range(3):
        nu = nu_ref[0, s]
        for c in range(2):
            d_sc[:, c] = d_all[c, nu].astype(F32).reshape(8, 8, LANES)
        flat = d_sc.reshape(2 * BLK, LANES)
        for b in range(2):
            rows = flat[pl.ds(b, BLK, stride=2), :]
            keep = jnp.where(lane < BLK, pat_ref[nu, 2 * b], pat_ref[nu, 2 * b + 1]) > 0
            d_nat[s * BLK : (s + 1) * BLK, b * LANES : (b + 1) * LANES] = jnp.where(keep, rows, 0.0)
    d_t[...] = d_nat[...].T.astype(BF16)

    @pl.loop(0, BLK // 2)
    def _(i):
        two = jnp.concatenate([tt[2 * i], tt[2 * i + 1]], axis=1)
        prod = jnp.dot(d_t[:, : 3 * BLK], two, preferred_element_type=F32)
        big[pl.ds(2 * i, 256, stride=BLK), :] = prod[:, :LANES]
        big[pl.ds(2 * i + 1, 256, stride=BLK), :] = prod[:, LANES:]

    def round_half(o):
        rows = big[pl.ds(pl.multiple_of(o * 512, 512), 512), :]
        half[o] = rows.astype(BF16).reshape(8, BLK, LANES)

    def far_copy(way, j, c, q, slot, where):
        sign = 1 - 2 * way
        o = 2 * ring(sign * (REACH + j)) + c
        cols = pl.ds(q * PAIR, PAIR)
        return remote(
            half.at[o, cols], far.at[way, slot, cols], f_snd.at[way, where, q], f_rcv.at[way, slot, q],
            (aux, 2 * ring(sign * j) + c),
        )

    def far_all(q):
        copies = []
        for c in range(2):
            copies.append(far_copy(core, REACH, c, q, 2 * REACH - 2, 2 * REACH - 2 + c))
            for j in range(REACH - 1, 0, -1):
                for way in range(2):
                    copies.append(far_copy(way, j, c, q, 2 * (j - 1) + core, 2 * (j - 1) + c))
        return copies

    @pl.loop(REACH + 1, chips - REACH)
    def _(e):
        for c in range(2):
            round_half(2 * ring(e) + c)

    @pl.loop(0, CHUNKS)
    def _(q):
        for copy in far_all(q):
            copy.start()

    def near_copy(e):
        return remote(half.at[2 * ring(e - REACH) + other], sib.at[e], n_snd.at[e], n_rcv.at[e], mate)

    @pl.loop(0, 2 * REACH + 1)
    def _(e):
        for c in range(2):
            round_half(2 * ring(e - REACH) + c)
        near_copy(e).start()

    @pl.loop(1, aux_n)
    def _(i):
        v_plane(i).wait_recv()

    v_mate.start()
    v_mate.wait_recv()

    def turned(first, second, put):
        for n, o in enumerate((first, second)):
            b = bm_ref[o]
            for c in range(2):
                v_sc[n, :, c] = v_all[c, b].astype(F32)
        flat = v_sc.reshape(2 * 4 * BLK, LANES)
        for b in range(4):
            rows = flat[pl.ds(b, 2 * BLK, stride=4), :]
            put(slice(b * LANES, (b + 1) * LANES), rows.T.astype(BF16))

    def put_own(rows, val):
        v_own[rows, :] = val
        for way in range(2):
            v_far[way, rows, 0:LANES] = val

    turned(orb, 2 * chip + other, put_own)
    for way in range(2):
        for j in range(1, REACH + 1):
            z = ring(-j if way == 0 else j)

            def put_far(rows, val):
                v_far[way, rows, j * LANES : (j + 1) * LANES] = val

            if j < REACH:
                turned(2 * z, 2 * z + 1, put_far)
            else:
                turned(2 * z + way, 2 * z + way, put_far)

    def own_blocks(e, q, k):
        lam = q * PAIR + k
        return [half[2 * ring(e) + core, lam], sib[e + REACH, lam]]

    def hop_copy(way, k, q):
        sign = 1 - 2 * way
        src = part.at[way, q] if k == 0 else hop.at[way, k - 1, q]
        return remote(src, hop.at[way, k, q], p_snd.at[way, k, q], p_rcv.at[way, k, q], (aux, 2 * ring(sign) + core))

    @pl.loop(0, 2 * REACH + 1)
    def _(e):
        near_copy(e).wait_recv()

    depth = (2 * REACH + 1) * BLK

    @pl.loop(0, CHUNKS)
    def _(q):
        for way in range(2):
            for slot in range(2 * REACH - 1):
                far_copy(way, 1, 0, q, slot, 0).wait_recv()
            cols = []
            for k in range(PAIR):
                blocks = own_blocks((1 - 2 * way) * REACH, q, k)
                blocks += [far[way, slot, q * PAIR + k] for slot in range(2 * REACH - 1)]
                cols.append(jnp.concatenate(blocks, axis=0))
            x = jnp.concatenate(cols, axis=1)
            part[way, q] = jnp.dot(v_far[way, :, :depth], x, preferred_element_type=F32).astype(BF16)
            hop_copy(way, 0, q).start()

    def own_term(e, q):
        x = jnp.concatenate([jnp.concatenate(own_blocks(e, q, k), axis=0) for k in range(PAIR)], axis=1)
        return jnp.dot(v_own[...], x, preferred_element_type=F32)

    for k in range(REACH - 1):
        @pl.loop(0, CHUNKS)
        def _(q):
            for way in range(2):
                hop_copy(way, k, q).wait_recv()
                e = (1 - 2 * way) * (REACH - 1 - k)
                total = own_term(e, q) + hop[way, k, q].astype(F32)
                hop[way, k, q] = total.astype(BF16)
                hop_copy(way, k + 1, q).start()

    @pl.loop(0, CHUNKS)
    def _(q):
        total = own_term(0, q)
        for way in range(2):
            hop_copy(way, REACH - 1, q).wait_recv()
            total += hop[way, REACH - 1, q].astype(F32)
        for k in range(PAIR):
            big[pl.ds(q * PAIR + k, 512, stride=8), :] = total[:, k * LANES : (k + 1) * LANES]

    @pl.loop(0, 16)
    def _(i):
        rows = pl.ds(pl.multiple_of(i * 256, 256), 256)
        out_ref[rows, :] = big[rows, :].astype(BF16)

    @pl.loop(1, chips)
    def _(i):
        d_along(i).wait_send()
        v_along(i).wait_send()

    @pl.loop(1, aux_n)
    def _(i):
        d_plane(i).wait_send()
        v_plane(i).wait_send()

    d_mate.wait_send()
    v_mate.wait_send()

    @pl.loop(0, 2 * REACH + 1)
    def _(e):
        near_copy(e).wait_send()

    @pl.loop(0, CHUNKS)
    def _(q):
        for copy in far_all(q):
            copy.wait_send()
        for way in range(2):
            for k in range(REACH):
                hop_copy(way, k, q).wait_send()


def on_device(tensor, nu_index, density, density_pattern, blockmap, virtual):
    aux_n, orb_n = lax.axis_size("aux"), lax.axis_size("orb")
    chips = orb_n // 2
    dma = pltpu.SemaphoreType.DMA
    vmem = pl.BlockSpec(memory_space=pltpu.VMEM)
    smem = pl.BlockSpec(memory_space=pltpu.SMEM)
    out = pl.pallas_call(
        functools.partial(kernel, aux_n, chips),
        out_shape=jax.ShapeDtypeStruct((512 * 8, LANES), BF16),
        in_specs=[smem, smem, smem, vmem, vmem, pl.BlockSpec(memory_space=pl.ANY)],
        out_specs=vmem,
        scratch_shapes=[
            pltpu.VMEM((3, BLK, BLK, LANES), BF16),
            pltpu.VMEM((256 * BLK, LANES), F32),
            pltpu.VMEM((BLK, 3 * BLK, LANES), BF16),
            pltpu.VMEM((16, LANES), F32),
            pltpu.VMEM((chips, 8, LANES), F32),
            pltpu.VMEM((2, 2 * aux_n, BLK, LANES), BF16),
            pltpu.VMEM((2, 2 * aux_n, chips // 2, 16, LANES), BF16),
            pltpu.VMEM((8, 2, 8, LANES), F32),
            pltpu.VMEM((2, 8, 2, 16, LANES), F32),
            pltpu.VMEM((4 * BLK, 2 * LANES), F32),
            pltpu.VMEM((2 * LANES, 4 * BLK), BF16),
            pltpu.VMEM((512, LANES), BF16),
            pltpu.VMEM((2, 512, (REACH + 1) * LANES), BF16),
            pltpu.VMEM((orb_n, 8, BLK, LANES), BF16),
            pltpu.VMEM((2, 2 * REACH - 1, 8, BLK, LANES), BF16),
            pltpu.VMEM((2 * REACH + 1, 8, BLK, LANES), BF16),
            pltpu.VMEM((2, CHUNKS, 512, PAIR * LANES), BF16),
            pltpu.VMEM((2, REACH, CHUNKS, 512, PAIR * LANES), BF16),
            dma,
            dma((2, chips)), dma((2, chips)),
            dma((2, aux_n)), dma((2, aux_n)),
            dma((2,)), dma((2,)),
            dma((2 * REACH + 1,)), dma((2 * REACH + 1,)),
            dma((2, 2 * REACH, CHUNKS)), dma((2, 2 * REACH, CHUNKS)),
            dma((2, REACH, CHUNKS)), dma((2, REACH, CHUNKS)),
        ],
        compiler_params=pltpu.CompilerParams(
            collective_id=0, has_side_effects=True, vmem_limit_bytes=56 * 2**20
        ),
        cost_estimate=pl.CostEstimate(flops=3 * 10**9, bytes_accessed=5 * 2**20, transcendentals=0),
        name="contract",
    )(nu_index, density_pattern, blockmap, density, virtual, tensor)
    return out.reshape(512, 8, LANES)


def solution(mesh):
    in_specs = (
        P("orb", None, None, "aux"),
        P("orb", None),
        P(("aux", "orb"), None),
        P(),
        P(),
        P(("aux", "orb"), None),
    )
    out_specs = P(None, "orb", "aux")
    return jax.shard_map(
        on_device, mesh=mesh, in_specs=in_specs, out_specs=out_specs, check_vma=False
    )
```

time: 473 us -> 193 us (0.41)
  waiting for transfers between devices: 418 us -> 0 us
  Pallas kernels: 0 us -> 189 us
  local copies, waits for them, and re-layouts: 24.7 us -> 3.63 us
  between operations: 15.4 us -> 0.01 us
  starting transfers between devices: 7.16 us -> 0 us
  matrix products: 6.79 us -> 0 us
    all_gather x2 -> x0, waiting for transfers between devices: 416 us -> none  [the longest x1 242 us: on_device(): virt_full = lax.all_gather(virtual, ('aux', 'orb'), axis=0, tiled=True)]
    pallas_call x0 -> x1, Pallas kernels: none -> 189 us  [on_device(): pl.pallas_call(functools.partial(kernel, aux_n, chips), out_shape=jax.Sha...]
    gather x2 -> x0, local copies, waits for them, and re-layouts: 8.35 us -> none  [on_device(): remapped.reshape(lam_local, orb_count, block_width, p_items)[:, inverse]]
    all_to_all x1 -> x0, starting transfers between devices: 7.12 us -> none  [on_device(): lax.all_to_all(half_done, 'orb', split_axis=0, concat_axis=1, tiled=True)]
    dot_general x2 -> x0, matrix products: 6.79 us -> none  [the longest x1 4.44 us: on_device(): lax.dot_general(chosen, flattened, (((0,), (0,)), ((), ())), preferred_el...]
    all_to_all x1 -> x0, local copies, waits for them, and re-layouts: 5.52 us -> none  [on_device(): lax.all_to_all(half_done, 'orb', split_axis=0, concat_axis=1, tiled=True)]
  transfers between devices with their start and end apart: 3 -> 0, of which waited for: 2 -> 0; matrix products, arithmetic and copies ran while one was open for 1% -> 0% of each run, Pallas kernels for 0% -> 0%
where the time goes in v1:
time: 193 us
  Pallas kernels  189 us (98%)
  local copies, waits for them, and re-layouts  3.63 us (2%)
    pallas_call x1, Pallas kernels, on_device(): pl.pallas_call(functools.partial(kernel, aux_n, chips), out_shape=jax.Sha...  189 us

profile of v1, /device:TPU:1, one launch (start us, length us, event | category | flops | bytes accessed | tf_op | source)
XLA Modules:
  0.0 193.0 jit_solution(11660768852063551367)
XLA Ops:
  0.0 1.4 copy.7.pat_ref
  1.4 189.3 %contract.1 = bf16[4096,128]{1,0:T(8,128)(2,1)} custom-call(s32[1,3]{1,0:T(1,128)} %nu_ref.1, s32[32,4]{1,0:T(8,128)} %copy.7.pat_ref, s32[32]{0:T(128)} %bm_ref.1, bf16[4,256]{1,0:T(4,128)(2,1)} %dens_ref.1, bf16[4,512]{1,0:T(4,128)(2,1)} %virt_ref.1, bf16[3,64,64,128]{3,2,1,0:T(8,128)(2,1)} %t_hbm.1), custom_call_target="tpu_custom_call" | custom-call | flops 3000000000 | bytes 5242880 | tf_op jit(solution)/shard_map/contract/pallas_call | solution.py:320
  190.7 2.3 %copy.9 = bf16[512,8,128]{2,1,0:T(8,128)(2,1)} copy(bf16[512,8,128]{2,1,0:T(8,128)(2,1)} %bitcast.1) | data formatting | bytes 2097152

commit v2 on v1

--- a/solution.py
+++ b/solution.py
@@ -20,7 +20,7 @@
 def kernel(
     aux_n, chips, nu_ref, pat_ref, bm_ref, dens_ref, virt_ref, t_hbm, out_ref,
     tbuf, big, tt, piece, d_in, d_all, v_all, d_sc, v_sc, d_nat, d_t, v_own, v_far,
-    half, far, sib, part, hop,
+    perm, mid, x_far, x_near, far, sib, part, hop,
     t_sem, a_snd, a_rcv, b_snd, b_rcv, c_snd, c_rcv, n_snd, n_rcv, f_snd, f_rcv, p_snd, p_rcv,
 ):
     aux = lax.axis_index("aux")
@@ -59,6 +59,10 @@
         greet((aux, 2 * ring(-j) + other))
     greet(mate)
 
+    row = lax.broadcasted_iota(jnp.int32, (256, 256), 0)
+    col = lax.broadcasted_iota(jnp.int32, (256, 256), 1)
+    perm[...] = jnp.where(row == lax.rem(col, 16) * 16 + lax.div(col, 16), 1.0, 0.0).astype(BF16)
+
     dens = dens_ref[...].astype(F32)
     for b in range(2):
         d_in[chip, pl.ds(b, 4, stride=2), :] = dens[:, b * LANES : (b + 1) * LANES]
@@ -77,13 +81,10 @@
         mine = v_all.at[core, 2 * aux + lax.div(chip, span), lax.rem(chip, span)]
         return remote(mine, mine, a_snd.at[1, i], a_rcv.at[1, i], (aux, 2 * ring(i) + core))
 
-    @pl.loop(1, chips)
-    def _(i):
-        d_along(i).start()
-
-    @pl.loop(1, chips)
-    def _(i):
-        v_along(i).start()
+    @pl.loop(0, chips - 1)
+    def _(i):
+        step = lax.div(i + 1, 2)
+        d_along(chips // 2 + step * (1 - 2 * lax.rem(i, 2))).start()
 
     load_t.wait()
 
@@ -116,7 +117,7 @@
 
     @pl.loop(1, chips)
     def _(i):
-        v_along(i).wait_recv()
+        v_along(i).start()
 
     @pl.loop(1, aux_n)
     def _(i):
@@ -125,6 +126,10 @@
     d_mate = remote(d_all.at[core], d_all.at[core], c_snd.at[0], c_rcv.at[0], mate)
     v_mate = remote(v_all.at[core], v_all.at[core], c_snd.at[1], c_rcv.at[1], mate)
     d_mate.start()
+
+    @pl.loop(1, chips)
+    def _(i):
+        v_along(i).wait_recv()
 
     @pl.loop(1, aux_n)
     def _(i):
@@ -141,27 +146,40 @@
         flat = d_sc.reshape(2 * BLK, LANES)
         for b in range(2):
             rows = flat[pl.ds(b, BLK, stride=2), :]
-            keep = jnp.where(lane < BLK, pat_ref[nu, 2 * b], pat_ref[nu, 2 * b + 1]) > 0
+            keep = jnp.where(lane < BLK, pat_ref[2 * b, nu], pat_ref[2 * b + 1, nu]) > 0
             d_nat[s * BLK : (s + 1) * BLK, b * LANES : (b + 1) * LANES] = jnp.where(keep, rows, 0.0)
-    d_t[...] = d_nat[...].T.astype(BF16)
-
-    @pl.loop(0, BLK // 2)
-    def _(i):
-        two = jnp.concatenate([tt[2 * i], tt[2 * i + 1]], axis=1)
-        prod = jnp.dot(d_t[:, : 3 * BLK], two, preferred_element_type=F32)
-        big[pl.ds(2 * i, 256, stride=BLK), :] = prod[:, :LANES]
-        big[pl.ds(2 * i + 1, 256, stride=BLK), :] = prod[:, LANES:]
-
-    def round_half(o):
-        rows = big[pl.ds(pl.multiple_of(o * 512, 512), 512), :]
-        half[o] = rows.astype(BF16).reshape(8, BLK, LANES)
+    turned_d = d_nat[...].T.astype(BF16)
+    for b in range(2):
+        d_t[b * 4 * BLK : (b + 1) * 4 * BLK, :] = turned_d
+
+    n_far, n_near = chips - 2 * REACH - 1, 2 * REACH + 1
+
+    def halves(first, count):
+        low = pl.multiple_of(lax.rem(16 * (chip + first), 16 * chips), 16)
+        lhs = d_t[pl.ds(low, 16 * count), : 3 * BLK]
+
+        @pl.loop(0, BLK // 2, unroll=4)
+        def _(i):
+            two = jnp.concatenate([tt[2 * i], tt[2 * i + 1]], axis=1)
+            prod = jnp.dot(lhs, two, preferred_element_type=F32).astype(BF16)
+            mid[2 * i, : 16 * count, :] = prod[:, :LANES]
+            mid[2 * i + 1, : 16 * count, :] = prod[:, LANES:]
+
+    def swap(g, put):
+        cols = pl.ds(pl.multiple_of(g * 16, 16), 16)
+        for i in range(0, 4, 2):
+            two = [mid[16 * n : 16 * n + 16, cols, :].reshape(256, LANES) for n in (i, i + 1)]
+            prod = jnp.dot(perm[...], jnp.concatenate(two, axis=1), preferred_element_type=F32).astype(BF16)
+            for n in range(2):
+                rows = slice(16 * (i + n), 16 * (i + n) + 16)
+                put(rows, prod[:, n * LANES : (n + 1) * LANES].reshape(2, 8, 16, LANES))
 
     def far_copy(way, j, c, q, slot, where):
         sign = 1 - 2 * way
-        o = 2 * ring(sign * (REACH + j)) + c
+        spot = sign * (REACH + j) + chips * way - REACH - 1
         cols = pl.ds(q * PAIR, PAIR)
         return remote(
-            half.at[o, cols], far.at[way, slot, cols], f_snd.at[way, where, q], f_rcv.at[way, slot, q],
+            x_far.at[spot, c, cols], far.at[way, slot, cols], f_snd.at[way, where, q], f_rcv.at[way, slot, q],
             (aux, 2 * ring(sign * j) + c),
         )
 
@@ -174,10 +192,14 @@
                     copies.append(far_copy(way, j, c, q, 2 * (j - 1) + core, 2 * (j - 1) + c))
         return copies
 
-    @pl.loop(REACH + 1, chips - REACH)
-    def _(e):
-        for c in range(2):
-            round_half(2 * ring(e) + c)
+    halves(REACH + 1, n_far)
+
+    @pl.loop(0, n_far)
+    def _(g):
+        def put(rows, val):
+            x_far[g, :, :, rows, :] = val
+
+        swap(g, put)
 
     @pl.loop(0, CHUNKS)
     def _(q):
@@ -185,12 +207,16 @@
             copy.start()
 
     def near_copy(e):
-        return remote(half.at[2 * ring(e - REACH) + other], sib.at[e], n_snd.at[e], n_rcv.at[e], mate)
-
-    @pl.loop(0, 2 * REACH + 1)
+        return remote(x_near.at[e, other], sib.at[e], n_snd.at[e], n_rcv.at[e], mate)
+
+    halves(chips - REACH, n_near)
+
+    @pl.loop(0, n_near)
     def _(e):
-        for c in range(2):
-            round_half(2 * ring(e - REACH) + c)
+        def put(rows, val):
+            x_near[e, :, :, rows, :] = val
+
+        swap(e, put)
         near_copy(e).start()
 
     @pl.loop(1, aux_n)
@@ -230,7 +256,7 @@
 
     def own_blocks(e, q, k):
         lam = q * PAIR + k
-        return [half[2 * ring(e) + core, lam], sib[e + REACH, lam]]
+        return [x_near[e + REACH, core, lam], sib[e + REACH, lam]]
 
     def hop_copy(way, k, q):
         sign = 1 - 2 * way
@@ -333,10 +359,13 @@
             pltpu.VMEM((8, 2, 8, LANES), F32),
             pltpu.VMEM((2, 8, 2, 16, LANES), F32),
             pltpu.VMEM((4 * BLK, 2 * LANES), F32),
-            pltpu.VMEM((2 * LANES, 4 * BLK), BF16),
+            pltpu.VMEM((4 * LANES, 4 * BLK), BF16),
             pltpu.VMEM((512, LANES), BF16),
             pltpu.VMEM((2, 512, (REACH + 1) * LANES), BF16),
-            pltpu.VMEM((orb_n, 8, BLK, LANES), BF16),
+            pltpu.VMEM((256, 256), BF16),
+            pltpu.VMEM((BLK, 16 * (2 * REACH + 1), LANES), BF16),
+            pltpu.VMEM((chips - 2 * REACH - 1, 2, 8, BLK, LANES), BF16),
+            pltpu.VMEM((2 * REACH + 1, 2, 8, BLK, LANES), BF16),
             pltpu.VMEM((2, 2 * REACH - 1, 8, BLK, LANES), BF16),
             pltpu.VMEM((2 * REACH + 1, 8, BLK, LANES), BF16),
             pltpu.VMEM((2, CHUNKS, 512, PAIR * LANES), BF16),
@@ -354,7 +383,7 @@
         ),
         cost_estimate=pl.CostEstimate(flops=3 * 10**9, bytes_accessed=5 * 2**20, transcendentals=0),
         name="contract",
-    )(nu_index, density_pattern, blockmap, density, virtual, tensor)
+    )(nu_index, density_pattern.T, blockmap, density, virtual, tensor)
     return out.reshape(512, 8, LANES)
 
 

time: 193 us -> 183 us (0.948)
  Pallas kernels: 189 us -> 181 us
    pallas_call x1, Pallas kernels: 189 us -> 181 us  [on_device(): pl.pallas_call(functools.partial(kernel, aux_n, chips), out_shape=jax.Sha...]
where the time goes in v2:
time: 183 us
  Pallas kernels  181 us (99%)
  local copies, waits for them, and re-layouts  2.26 us (1%)
    pallas_call x1, Pallas kernels, on_device(): pl.pallas_call(functools.partial(kernel, aux_n, chips), out_shape=jax.Sha...  181 us

profile of v2, /device:TPU:1, one launch (start us, length us, event | category | flops | bytes accessed | tf_op | source)
XLA Modules:
  0.0 183.0 jit_solution(14493476359288358403)
XLA Ops:
  0.0 180.7 %contract.1 = bf16[4096,128]{1,0:T(8,128)(2,1)} custom-call(s32[1,3]{1,0:T(1,128)} %nu_ref.1, s32[4,32]{1,0:T(4,128)} %bitcast.3, s32[32]{0:T(128)} %bm_ref.1, bf16[4,256]{1,0:T(4,128)(2,1)} %dens_ref.1, bf16[4,512]{1,0:T(4,128)(2,1)} %virt_ref.1, bf16[3,64,64,128]{3,2,1,0:T(8,128)(2,1)} %t_hbm.1), custom_call_target="tpu_custom_call" | custom-call | flops 3000000000 | bytes 5242880 | tf_op jit(solution)/shard_map/contract/pallas_call | solution.py:346
  180.7 2.3 %copy.8 = bf16[512,8,128]{2,1,0:T(8,128)(2,1)} copy(bf16[512,8,128]{2,1,0:T(8,128)(2,1)} %bitcast.2) | data formatting | bytes 2097152

commit v3 on v0

v3 whole, which is shorter than its diff:
```python
import functools

import jax
import jax.numpy as jnp
from jax import lax
from jax.experimental import pallas as pl
from jax.experimental.pallas import tpu as pltpu
from jax.sharding import PartitionSpec as P

MESH = pl.DeviceIdType.MESH
BF16 = jnp.bfloat16
F32 = jnp.float32
BLK = 64
LANES = 128
REACH = 4
CHUNKS = 4
PAIR = 2


def kernel(
    aux_n, chips, nu_ref, pat_ref, bm_ref, dens_ref, virt_ref, t_hbm, out_ref,
    tbuf, big, tt, piece, nu_out, nu_in, nu_mate, pair_of, d_out, d_in, d_rot, d_first, d_second, d_t, v_all, v_sc, v_own, v_far,
    perm, mid, x, far, far_end, part, hop,
    t_sem, n_sem, a_snd, a_rcv, e_snd, e_rcv, b_snd, b_rcv, w_snd, w_rcv, m_snd, m_rcv, f_snd, f_rcv, p_snd, p_rcv,
):
    aux = lax.axis_index("aux")
    orb = lax.axis_index("orb")
    chip = lax.div(orb, 2)
    core = lax.rem(orb, 2)
    other = 1 - core
    mate = (aux, 2 * chip + other)

    def wrap(at, n):
        return jnp.where(at >= n, at - n, jnp.where(at < 0, at + n, at))

    def ring(shift):
        return wrap(chip + shift, chips)

    def remote(src, dst, snd, rcv, to):
        return pltpu.make_async_remote_copy(
            src_ref=src, dst_ref=dst, send_sem=snd, recv_sem=rcv, device_id=to, device_id_type=MESH
        )

    load_t = pltpu.make_async_copy(t_hbm, tbuf, t_sem)
    load_t.start()

    barrier = pltpu.get_barrier_semaphore()

    def greet(to):
        pl.semaphore_signal(barrier, inc=1, device_id=to, device_id_type=MESH)

    rings = [ring(i) for i in range(-REACH, REACH + 1)]

    def along(act):
        act(ring(chips // 2))

        @pl.loop(1, chips // 2)
        def _(i):
            act(ring(chips // 2 - i))
            act(ring(i - chips // 2))

    def across(act):
        @pl.loop(1, aux_n)
        def _(i):
            act(wrap(aux + i, aux_n))

    def greet_chip(z):
        for c in range(2):
            greet((aux, 2 * z + c))

    along(greet_chip)
    greet(mate)
    across(lambda a: greet((a, orb)))

    row = lax.broadcasted_iota(jnp.int32, (256, 256), 0)
    col = lax.broadcasted_iota(jnp.int32, (256, 256), 1)
    perm[...] = jnp.where(row == lax.rem(col, 16) * 16 + lax.div(col, 16), 1.0, 0.0).astype(BF16)

    dens = dens_ref[...].astype(F32)
    d_rot[0:4, :] = dens[:, :LANES]
    d_rot[4:8, :] = dens[:, :LANES]
    d_rot[8:12, :] = dens[:, LANES:]
    d_rot[12:16, :] = dens[:, LANES:]
    mine = lax.div(lax.broadcasted_iota(jnp.int32, (8, LANES), 0), 4) == core
    left, right = (jnp.where(mine, d_rot[8 * b : 8 * b + 8, :], 0.0) for b in range(2))
    took = lax.broadcasted_iota(jnp.int32, (LANES, LANES), 0)
    gives = lax.broadcasted_iota(jnp.int32, (LANES, LANES), 1)
    for c in range(2):
        want = lax.div(gives, 8) * 16 + 8 * c + lax.rem(gives, 8)
        d_out[c] = jnp.dot(left, jnp.where(took == want, 1.0, 0.0), preferred_element_type=F32) + jnp.dot(
            right, jnp.where(took + LANES == want, 1.0, 0.0), preferred_element_type=F32
        )
    d_in[2 * chip + core] = d_out[core]
    line = lax.broadcasted_iota(jnp.int32, (8, LANES), 0)
    nu_out[...] = jnp.where(line == 0, nu_ref[0, 0], jnp.where(line == 1, nu_ref[0, 1], nu_ref[0, 2]))
    for n in range(2 * aux_n):
        pair_of[n] = n // 2

    virt = virt_ref[...].astype(F32)
    for b in range(4):
        piece[pl.ds(b, 4, stride=4), :] = virt[:, b * LANES : (b + 1) * LANES]
    v_all[core, aux, chip] = piece[...].astype(BF16)

    load_t.wait()

    @pl.loop(0, 3 * BLK // 8)
    def _(i):
        rows = tbuf[lax.div(i, 8), pl.ds(lax.rem(i, 8) * 8, 8)]
        big[pl.ds(pl.multiple_of(i * 512, 512), 512), :] = rows.astype(F32).reshape(512, LANES)

    @pl.loop(0, BLK)
    def _(m):
        tt[core, m] = big[pl.ds(m, 3 * BLK, stride=BLK), :].astype(BF16)

    pl.semaphore_wait(barrier, (2 * chips - 1) + (aux_n - 1))

    def d_sent(z, c):
        at = d_in.at[2 * chip + core]
        return remote(d_out.at[c], at, a_snd.at[2 * z + c], a_rcv.at[2 * chip + core], (aux, 2 * z + c))

    def d_came(z, c):
        return remote(d_out.at[0], d_in.at[2 * z + c], a_snd.at[0], a_rcv.at[2 * z + c], mate)

    def both_cores(act):
        def on_chip(z):
            for c in range(2):
                act(z, c)

        along(on_chip)
        act(chip, other)

    both_cores(lambda z, c: d_sent(z, c).start())

    t_mate = remote(tt.at[core], tt.at[core], m_snd.at[0], m_rcv.at[0], mate)
    nu_copy = remote(nu_out, nu_in, m_snd.at[1], m_rcv.at[1], mate)
    nu_copy.start()
    t_mate.start()

    both_cores(lambda z, c: d_came(z, c).wait_recv())

    rows = (lambda two: two[:, 0] + two[:, 1])(d_in[...].reshape(chips, 2, 8, LANES)).reshape(2 * BLK, LANES).T
    for b in range(2):
        d_rot[b * LANES : (b + 1) * LANES, :] = rows
    first = pl.multiple_of(8 * ring(REACH + 1), 8)
    turned_d = d_rot[pl.ds(first, LANES), :].astype(BF16)
    d_parts = (d_first, d_second)
    for h in range(2):
        d_parts[h][aux] = turned_d[h * BLK : (h + 1) * BLK]

    def d_over(h, a):
        mine_d = d_parts[h].at[aux]
        return remote(mine_d, mine_d, b_snd.at[h, a], b_rcv.at[h, aux], (a, orb))

    def d_from(h, a):
        theirs = d_parts[h].at[a]
        return remote(theirs, theirs, b_snd.at[h, a], b_rcv.at[h, a], (a, orb))

    across(lambda a: d_over(0, a).start())

    def v_sent(z):
        mine_v = v_all.at[core, aux, chip]
        return remote(mine_v, mine_v, e_snd.at[z], e_rcv.at[chip], (aux, 2 * z + core))

    def v_came(z):
        theirs = v_all.at[core, aux, z]
        return remote(theirs, theirs, e_snd.at[z], e_rcv.at[z], mate)

    along(lambda z: v_sent(z).start())

    def v_over(a):
        mine_v = v_all.at[core, aux]
        return remote(mine_v, mine_v, w_snd.at[a], w_rcv.at[aux], (a, orb))

    def v_from(a):
        theirs = v_all.at[core, a]
        return remote(theirs, theirs, w_snd.at[a], w_rcv.at[a], (a, orb))

    v_mate = remote(v_all.at[core], v_all.at[core], m_snd.at[2], m_rcv.at[2], mate)

    nu_copy.wait_recv()
    nu_local = pltpu.make_async_copy(nu_in, nu_mate, n_sem)
    nu_local.start()
    nu_local.wait()
    t_mate.wait_recv()

    def choose(h):
        across(lambda a: d_from(h, a).wait_recv())
        spot = lax.div(lax.broadcasted_iota(jnp.int32, (BLK, BLK), 0), 8) + (8 * h + REACH + 1 + chip)
        group = lax.div(lax.rem(spot, chips), 4)
        for n in range(2):
            for s in range(3):
                nu = jnp.where(core == n, nu_ref[0, s], nu_mate[s, 0])
                at = pair_of[nu]
                both = d_parts[h][at].astype(F32)
                rows = jnp.where(nu == 2 * at, both[:, :BLK], both[:, BLK:])
                keep = jnp.where(group < 2, jnp.where(group == 0, pat_ref[0, nu], pat_ref[1, nu]),
                                 jnp.where(group == 2, pat_ref[2, nu], pat_ref[3, nu])) > 0
                d_t[h, n, :, s * BLK : (s + 1) * BLK] = jnp.where(keep, rows, 0.0).astype(BF16)

    def halves(h, order, ready):
        @pl.loop(0, BLK // 2, unroll=4)
        def _(i):
            for n in range(2):
                two = jnp.concatenate([tt[n, 2 * i], tt[n, 2 * i + 1]], axis=1)
                prod = jnp.dot(d_t[h, n, :, : 3 * BLK], two, preferred_element_type=F32).astype(BF16)
                mid[n * BLK + 2 * i] = prod[:, :LANES]
                mid[n * BLK + 2 * i + 1] = prod[:, LANES:]

        for g in order:
            cols = slice(g * 16, g * 16 + 16)
            for i in range(0, 8, 2):
                two = [mid[16 * n : 16 * n + 16, cols, :].reshape(256, LANES) for n in (i, i + 1)]
                prod = jnp.dot(perm[...], jnp.concatenate(two, axis=1), preferred_element_type=F32).astype(BF16)
                for n in range(2):
                    val = prod[:, n * LANES : (n + 1) * LANES].reshape(2, 8, 16, LANES)
                    x[8 * h + 2 * g : 8 * h + 2 * g + 2, :, 16 * (i + n) : 16 * (i + n) + 16, :] = val
            ready(g)

    def spot_of(e):
        return (e - REACH - 1) % chips

    def far_copy(way, j, q):
        sign = 1 - 2 * way
        cols = pl.ds(q * PAIR, PAIR)
        src = x.at[spot_of(sign * (REACH + j)), cols]
        dst = far.at[way, min(j, REACH - 1) - 1, cols]
        if j == REACH:
            src = x.at[spot_of(sign * (REACH + j)), cols, pl.ds(way * BLK, BLK)]
            dst = far_end.at[way, cols]
        return remote(src, dst, f_snd.at[way, j - 1, q], f_rcv.at[way, j - 1, q], (aux, 2 * rings[REACH + sign * j] + core))

    def send_far(g):
        for way in range(2):
            for j in range(REACH, 0, -1):
                if spot_of((1 - 2 * way) * (REACH + j)) // 2 == g:
                    pl.loop(0, CHUNKS)(lambda q: far_copy(way, j, q).start())

    choose(0)
    halves(0, (1, 0, 2, 3), send_far)

    across(lambda a: d_over(1, a).start())
    along(lambda z: v_came(z).wait_recv())
    across(lambda a: v_over(a).start())

    choose(1)
    halves(1, range(4), lambda g: None)

    across(lambda a: v_from(a).wait_recv())
    v_mate.start()
    v_mate.wait_recv()

    v_blocks = v_all.reshape(2, 2 * aux_n, chips // 2, 16, LANES)

    def turned(first, second, put):
        for n, o in enumerate((first, second)):
            b = bm_ref[o]
            for c in range(2):
                v_sc[n, :, c] = v_blocks[c, b].astype(F32)
        flat = v_sc.reshape(2 * 4 * BLK, LANES)
        for b in range(4):
            rows = flat[pl.ds(b, 2 * BLK, stride=4), :]
            put(slice(b * LANES, (b + 1) * LANES), rows.T.astype(BF16))

    def put_own(rows, val):
        v_own[rows, :] = val
        for way in range(2):
            v_far[way, rows, 0:LANES] = val

    turned(2 * chip, 2 * chip + 1, put_own)
    for way in range(2):
        for j in range(1, REACH + 1):
            z = rings[REACH + (-j if way == 0 else j)]

            def put_far(rows, val):
                v_far[way, rows, j * LANES : (j + 1) * LANES] = val

            if j < REACH:
                turned(2 * z, 2 * z + 1, put_far)
            else:
                turned(2 * z + way, 2 * z + way, put_far)

    both_cores(lambda z, c: d_sent(z, c).wait_send())
    along(lambda z: v_sent(z).wait_send())
    for h in range(2):
        across(lambda a: d_over(h, a).wait_send())
    across(lambda a: v_over(a).wait_send())
    t_mate.wait_send()
    nu_copy.wait_send()
    v_mate.wait_send()

    def hop_copy(way, k, q):
        sign = 1 - 2 * way
        src = part.at[way, q] if k == 0 else hop.at[way, k - 1, q]
        return remote(src, hop.at[way, k, q], p_snd.at[way, k, q], p_rcv.at[way, k, q], (aux, 2 * rings[REACH + sign] + core))

    depth = (2 * REACH + 1) * BLK

    @pl.loop(0, CHUNKS)
    def _(q):
        for way in range(2):
            for j in range(1, REACH + 1):
                far_copy(way, j, q).wait_recv()
            cols = []
            for k in range(PAIR):
                lam = q * PAIR + k
                blocks = [x[spot_of((1 - 2 * way) * REACH), lam]]
                blocks += [far[way, j, lam] for j in range(REACH - 1)] + [far_end[way, lam]]
                cols.append(jnp.concatenate(blocks, axis=0))
            terms = jnp.concatenate(cols, axis=1)
            part[way, q] = jnp.dot(v_far[way, :, :depth], terms, preferred_element_type=F32).astype(BF16)
            hop_copy(way, 0, q).start()

    def own_term(e, q):
        terms = jnp.concatenate([x[spot_of(e), q * PAIR + k] for k in range(PAIR)], axis=1)
        return jnp.dot(v_own[...], terms, preferred_element_type=F32)

    for k in range(REACH - 1):
        @pl.loop(0, CHUNKS)
        def _(q):
            for way in range(2):
                hop_copy(way, k, q).wait_recv()
                e = (1 - 2 * way) * (REACH - 1 - k)
                total = own_term(e, q) + hop[way, k, q].astype(F32)
                hop[way, k, q] = total.astype(BF16)
                hop_copy(way, k + 1, q).start()
                hop_copy(way, k, q).wait_send()
                if k == 0:
                    for j in range(1, REACH + 1):
                        far_copy(way, j, q).wait_send()

    @pl.loop(0, CHUNKS)
    def _(q):
        total = own_term(0, q)
        for way in range(2):
            hop_copy(way, REACH - 1, q).wait_recv()
            total += hop[way, REACH - 1, q].astype(F32)
            hop_copy(way, REACH - 1, q).wait_send()
        for k in range(PAIR):
            big[pl.ds(q * PAIR + k, 512, stride=8), :] = total[:, k * LANES : (k + 1) * LANES]

    @pl.loop(0, 16, unroll=4)
    def _(i):
        rows = pl.ds(pl.multiple_of(i * 256, 256), 256)
        out_ref[rows, :] = big[rows, :].astype(BF16)


def on_device(tensor, nu_index, density, density_pattern, blockmap, virtual):
    aux_n, orb_n = lax.axis_size("aux"), lax.axis_size("orb")
    chips = orb_n // 2
    dma = pltpu.SemaphoreType.DMA
    vmem = pl.BlockSpec(memory_space=pltpu.VMEM)
    smem = pl.BlockSpec(memory_space=pltpu.SMEM)
    out = pl.pallas_call(
        functools.partial(kernel, aux_n, chips),
        out_shape=jax.ShapeDtypeStruct((512 * 8, LANES), BF16),
        in_specs=[smem, smem, smem, vmem, vmem, pl.BlockSpec(memory_space=pl.ANY)],
        out_specs=vmem,
        scratch_shapes=[
            pltpu.VMEM((3, BLK, BLK, LANES), BF16),
            pltpu.VMEM((3 * BLK * BLK, LANES), F32),
            pltpu.VMEM((2, BLK, 3 * BLK, LANES), BF16),
            pltpu.VMEM((16, LANES), F32),
            pltpu.VMEM((8, LANES), jnp.int32),
            pltpu.VMEM((8, LANES), jnp.int32),
            pltpu.SMEM((8, LANES), jnp.int32),
            pltpu.SMEM((2 * aux_n,), jnp.int32),
            pltpu.VMEM((2, 8, LANES), F32),
            pltpu.VMEM((2 * chips, 8, LANES), F32),
            pltpu.VMEM((2 * LANES, LANES), F32),
            pltpu.VMEM((aux_n, BLK, LANES), BF16),
            pltpu.VMEM((aux_n, BLK, LANES), BF16),
            pltpu.VMEM((2, 2, BLK, 4 * BLK), BF16),
            pltpu.VMEM((2, aux_n, chips, 16, LANES), BF16),
            pltpu.VMEM((2, 8, 2, 16, LANES), F32),
            pltpu.VMEM((512, LANES), BF16),
            pltpu.VMEM((2, 512, (REACH + 1) * LANES), BF16),
            pltpu.VMEM((256, 256), BF16),
            pltpu.VMEM((2 * BLK, BLK, LANES), BF16),
            pltpu.VMEM((chips, 8, 2 * BLK, LANES), BF16),
            pltpu.VMEM((2, REACH - 1, 8, 2 * BLK, LANES), BF16),
            pltpu.VMEM((2, 8, BLK, LANES), BF16),
            pltpu.VMEM((2, CHUNKS, 512, PAIR * LANES), BF16),
            pltpu.VMEM((2, REACH, CHUNKS, 512, PAIR * LANES), BF16),
            dma, dma,
            dma((2 * chips,)), dma((2 * chips,)),
            dma((chips,)), dma((chips,)),
            dma((2, aux_n)), dma((2, aux_n)),
            dma((aux_n,)), dma((aux_n,)),
            dma((3,)), dma((3,)),
            dma((2, REACH, CHUNKS)), dma((2, REACH, CHUNKS)),
            dma((2, REACH, CHUNKS)), dma((2, REACH, CHUNKS)),
        ],
        compiler_params=pltpu.CompilerParams(
            collective_id=0, has_side_effects=True, vmem_limit_bytes=56 * 2**20
        ),
        cost_estimate=pl.CostEstimate(flops=3 * 10**9, bytes_accessed=5 * 2**20, transcendentals=0),
        name="contract",
    )(nu_index, density_pattern.T, blockmap, density, virtual, tensor)
    return out.reshape(512, 8, LANES)


def solution(mesh):
    in_specs = (
        P("orb", None, None, "aux"),
        P("orb", None),
        P(("aux", "orb"), None),
        P(),
        P(),
        P(("aux", "orb"), None),
    )
    out_specs = P(None, "orb", "aux")
    return jax.shard_map(
        on_device, mesh=mesh, in_specs=in_specs, out_specs=out_specs, check_vma=False
    )
```

time: 473 us -> 183 us (0.39)
  waiting for transfers between devices: 418 us -> 0 us
  Pallas kernels: 0 us -> 181 us
  local copies, waits for them, and re-layouts: 24.7 us -> 2.26 us
  between operations: 15.4 us -> 0.01 us
  starting transfers between devices: 7.16 us -> 0 us
  matrix products: 6.79 us -> 0 us
    all_gather x2 -> x0, waiting for transfers between devices: 416 us -> none  [the longest x1 242 us: on_device(): virt_full = lax.all_gather(virtual, ('aux', 'orb'), axis=0, tiled=True)]
    pallas_call x0 -> x1, Pallas kernels: none -> 181 us  [on_device(): pl.pallas_call(functools.partial(kernel, aux_n, chips), out_shape=jax.Sha...]
    gather x2 -> x0, local copies, waits for them, and re-layouts: 8.35 us -> none  [on_device(): remapped.reshape(lam_local, orb_count, block_width, p_items)[:, inverse]]
    all_to_all x1 -> x0, starting transfers between devices: 7.12 us -> none  [on_device(): lax.all_to_all(half_done, 'orb', split_axis=0, concat_axis=1, tiled=True)]
    dot_general x2 -> x0, matrix products: 6.79 us -> none  [the longest x1 4.44 us: on_device(): lax.dot_general(chosen, flattened, (((0,), (0,)), ((), ())), preferred_el...]
    all_to_all x1 -> x0, local copies, waits for them, and re-layouts: 5.52 us -> none  [on_device(): lax.all_to_all(half_done, 'orb', split_axis=0, concat_axis=1, tiled=True)]
    unnamed x6 -> x1, local copies, waits for them, and re-layouts: 7.71 us -> 2.26 us
  transfers between devices with their start and end apart: 3 -> 0, of which waited for: 2 -> 0; matrix products, arithmetic and copies ran while one was open for 1% -> 0% of each run, Pallas kernels for 0% -> 0%
where the time goes in v3:
time: 183 us
  Pallas kernels  181 us (99%)
  local copies, waits for them, and re-layouts  2.26 us (1%)
    pallas_call x1, Pallas kernels, on_device(): pl.pallas_call(functools.partial(kernel, aux_n, chips), out_shape=jax.Sha...  181 us

profile of v3, /device:TPU:1, one launch (start us, length us, event | category | flops | bytes accessed | tf_op | source)
XLA Modules:
  0.0 183.1 jit_solution(10815373056708859427)
XLA Ops:
  0.0 180.9 %contract.1 = bf16[4096,128]{1,0:T(8,128)(2,1)} custom-call(s32[1,3]{1,0:T(1,128)} %nu_ref.1, s32[4,32]{1,0:T(4,128)} %bitcast.3, s32[32]{0:T(128)} %bm_ref.1, bf16[4,256]{1,0:T(4,128)(2,1)} %dens_ref.1, bf16[4,512]{1,0:T(4,128)(2,1)} %virt_ref.1, bf16[3,64,64,128]{3,2,1,0:T(8,128)(2,1)} %t_hbm.1), custom_call_target="tpu_custom_call" | custom-call | flops 3000000000 | bytes 5242880 | tf_op jit(solution)/shard_map/contract/pallas_call | solution.py:353
  180.9 2.3 %copy.8 = bf16[512,8,128]{2,1,0:T(8,128)(2,1)} copy(bf16[512,8,128]{2,1,0:T(8,128)(2,1)} %bitcast.2) | data formatting | bytes 2097152
